TPU v7x, 512 devices: a whole 4x4x16 slice. The times are simulated.
512 devices in a mesh: section: 16 (over y, x), tm: 32 (over z, core).
Axes of the slice: x: 4, y: 4, z: 16, core: 2. Of those that a mesh axis runs over, the one named last changes fastest.
Arguments:
- series: bfloat16 [7, 4096, 1024], P(None, 'tm', 'section'), may hold values from -6 to 6
- query_key_value_weight: bfloat16 [16, 1024, 1536], P('section'), may hold values from -1.25 to 1.25, as said below
- output_weight: bfloat16 [16, 512, 1024], P('section'), may hold values from -0.25 to 0.25
- gain: float32 [16, 1024], P('section'), may hold values from 0.5 to 1.5
- readout_weight: float32 [16, 1024], P('section'), may hold values from -0.046875 to 0.046875
- dilation_block: int32 [64], replicated, may hold values from 0 to 1
- order: int32 [7], replicated, may hold values from 0 to 6, each once
Outputs:
- rul: float32 [7, 32, 128], P(None, 'tm', 'section')
Inputs may be any that keep to these rules, and one draw needn't show every extreme that they name: `query_key_value_weight`: entries of order the inverse square root of 1024. `order`: A permutation of the slots.
All inputs are finite; a program needn't handle non-finite values.
Results may differ from a plain program's by a relative error of at most 0.025.
Values may be sent and summed in bfloat16 or wider, within the bound.
A program may use at most 64 MiB of HBM per device.

v0:
```python
import jax
import jax.numpy as jnp
from jax import lax
from jax.sharding import PartitionSpec as P

HEADS_L = 4
HEADS_D = 4
HD = 64
WINDOW = 256
BLK = 64
EPSILON = 1e-05


def from_behind(value, axis, steps):
    count = lax.axis_size(axis)
    leading, last = (max(0, -steps), min(count, count - steps))
    return lax.ppermute(value, axis, [(source, source + steps) for source in range(leading, last)])


def passed_along(value, axis, steps):
    count = lax.axis_size(axis)
    pairs = [(source, (source + steps) % count) for source in range(count)]
    return lax.ppermute(value, axis, pairs)


def norm_rows(values):
    return values * lax.rsqrt(jnp.mean(values * values, axis=-1, keepdims=True) + EPSILON)


def soft_weights(scores, allowed):
    if allowed is not None:
        scores = jnp.where(allowed, scores, -1e30)
    top_score = jnp.max(scores, axis=-1, keepdims=True)
    raised = jnp.exp(scores - top_score)
    return (raised / jnp.sum(raised, axis=-1, keepdims=True)).astype(jnp.bfloat16)


def local(
    series, query_key_value_weight, output_weight, gain, readout_weight, dilation_block, order
):
    section_id = lax.axis_index("section")
    section_count = lax.axis_size("section")
    my_shard = lax.axis_index("tm")
    shard_count = lax.axis_size("tm")
    half_away = shard_count // 2
    micro_count = series.shape[0]
    row_count = series.shape[1]
    model_width = query_key_value_weight.shape[1]
    weight_qkv = query_key_value_weight[0]
    weight_out = output_weight[0]
    norm_gain = gain[0]
    read_vector = readout_weight[0]
    local_width = HEADS_L * HD
    dilated_width = HEADS_D * HD
    head_width = local_width + dilated_width
    block_total = row_count // BLK
    score_scale = HD ** (-0.5)
    highest = lax.Precision.HIGHEST
    tick_count = micro_count + section_count - 1
    span_count = max(1, WINDOW // row_count)
    wanted_shard = (my_shard + half_away) % shard_count
    wanted_blocks = lax.dynamic_slice_in_dim(
        dilation_block, wanted_shard * block_total, block_total, 0
    )
    query_pos = my_shard * row_count + jnp.arange(row_count, dtype=jnp.int32)
    key_pos = my_shard * row_count - WINDOW + jnp.arange(WINDOW + row_count, dtype=jnp.int32)
    window_mask = (
        (key_pos[None, :] > query_pos[:, None] - WINDOW)
        & (key_pos[None, :] <= query_pos[:, None])
        & (key_pos[None, :] >= 0)
    )

    def project(hidden):
        normed = (norm_rows(hidden.astype(jnp.float32)) * norm_gain).astype(jnp.bfloat16)
        return jnp.dot(normed, weight_qkv, preferred_element_type=jnp.float32)

    def skip_project(hidden):
        return jnp.zeros((row_count, 3 * head_width), jnp.float32)

    def attend(operands):
        hidden, projected, window_kv, far_kv = operands
        query_cols = projected[:, :head_width]
        key_cols = projected[:, head_width : 2 * head_width]
        value_cols = projected[:, 2 * head_width :]
        near_keys = jnp.concatenate(
            [window_kv[:, :local_width], key_cols[:, :local_width]], axis=0
        ).reshape(WINDOW + row_count, HEADS_L, HD)
        near_values = jnp.concatenate(
            [window_kv[:, local_width:], value_cols[:, :local_width]], axis=0
        ).reshape(WINDOW + row_count, HEADS_L, HD)
        near_queries = query_cols[:, :local_width].reshape(row_count, HEADS_L, HD)
        near_scores = (
            jnp.einsum("qhd,khd->hqk", near_queries, near_keys, precision=highest) * score_scale
        )
        near_weights = soft_weights(near_scores, window_mask[None])
        near_out = jnp.einsum(
            "hqk,khd->qhd", near_weights.astype(jnp.float32), near_values, precision=highest
        ).reshape(row_count, local_width)
        far_queries = query_cols[:, local_width:].reshape(block_total, BLK, HEADS_D, HD)
        own_keys = key_cols[:, local_width:].reshape(block_total, BLK, HEADS_D, HD)
        own_values = value_cols[:, local_width:].reshape(block_total, BLK, HEADS_D, HD)
        far_all = far_kv.reshape(block_total, BLK, 2 * dilated_width)
        far_keys = jnp.concatenate(
            [own_keys, far_all[:, :, :dilated_width].reshape(block_total, BLK, HEADS_D, HD)], axis=1
        )
        far_values = jnp.concatenate(
            [own_values, far_all[:, :, dilated_width:].reshape(block_total, BLK, HEADS_D, HD)],
            axis=1,
        )
        far_scores = (
            jnp.einsum("nqhd,nkhd->nhqk", far_queries, far_keys, precision=highest) * score_scale
        )
        far_weights = soft_weights(far_scores, None)
        far_out = jnp.einsum(
            "nhqk,nkhd->nqhd", far_weights.astype(jnp.float32), far_values, precision=highest
        ).reshape(row_count, dilated_width)
        heads_out = jnp.concatenate([near_out, far_out], axis=1).astype(jnp.bfloat16)
        updated = (
            hidden.astype(jnp.float32)
            + jnp.dot(heads_out, weight_out, preferred_element_type=jnp.float32)
        ).astype(jnp.bfloat16)
        readout = jnp.sum(norm_rows(updated.astype(jnp.float32)) * read_vector, axis=1)
        return (updated, readout)

    def skip_attend(operands):
        return (operands[0], jnp.zeros((row_count,), jnp.float32))

    def run_tick(tick_index, incoming_state, totals, first_input):
        slot_index = tick_index - section_id
        active = (slot_index >= 0) & (slot_index < micro_count)
        clipped = jnp.clip(slot_index, 0, micro_count - 1)
        hidden = jnp.where(section_id == 0, first_input, incoming_state)
        projected = lax.cond(active, project, skip_project, hidden)
        local_kv = jnp.concatenate(
            [
                projected[:, head_width : head_width + local_width],
                projected[:, 2 * head_width : 2 * head_width + local_width],
            ],
            axis=1,
        )
        pieces = []
        for distance in range(1, span_count + 1):
            pieces.append(from_behind(local_kv, "tm", distance))
        window_kv = jnp.concatenate(pieces[::-1], axis=0)
        far_local = jnp.concatenate(
            [
                projected[:, head_width + local_width : 2 * head_width],
                projected[:, 2 * head_width + local_width :],
            ],
            axis=1,
        )
        outgoing = far_local.reshape(block_total, BLK, 2 * dilated_width)[wanted_blocks].reshape(
            row_count, 2 * dilated_width
        )
        far_kv = passed_along(outgoing, "tm", half_away)
        updated, readout = lax.cond(
            active, attend, skip_attend, (hidden, projected, window_kv, far_kv)
        )
        picker = (jnp.arange(micro_count, dtype=jnp.int32) == clipped).astype(jnp.float32)
        totals = totals + picker[:, None] * readout[None, :]
        passed_on = from_behind(updated, "section", 1)
        return (passed_on, totals)

    initial = (
        jnp.zeros((row_count, model_width), jnp.bfloat16),
        jnp.zeros((micro_count, row_count), jnp.float32),
    )
    whole_series = lax.all_gather(series, "section", axis=2, tiled=True)

    def tick_all(tick_index, carry):
        slot_here = jnp.clip(tick_index, 0, micro_count - 1)
        picked = lax.dynamic_index_in_dim(order, slot_here, 0, keepdims=False)
        first_input = lax.dynamic_index_in_dim(whole_series, picked, 0, keepdims=False)
        return run_tick(tick_index, carry[0], carry[1], first_input)

    final_state, totals = lax.fori_loop(0, tick_count, tick_all, initial)
    shares = lax.psum_scatter(totals, "section", scatter_dimension=1, tiled=True)
    return shares.reshape(micro_count, 1, row_count // section_count)


def solution(mesh):
    placed = (
        P(None, "tm", "section"),
        P("section", None, None),
        P("section", None, None),
        P("section", None),
        P("section", None),
        P(),
        P(),
    )
    return jax.shard_map(
        local, mesh=mesh, in_specs=placed, out_specs=P(None, "tm", "section"), check_vma=False
    )
```

profile of v0, /device:TPU:64, one launch (start us, length us, event | category | flops | bytes accessed | tf_op | source)
XLA Modules:
  0.0 1573.4 jit_solution(16294063501692997884)
XLA Ops:
  11.2 62.6 %all-gather.2.cloned.1.call-done = bf16[7,128,1024]{1,2,0:T(8,128)(2,1)} async-done(((bf16[7,128,64]{1,2,0:T(8,128)(2,1)}), bf16[7,128,1024]{1,2,0:T(8,128)(2,1)}) %all-gather.2.cloned.1.call-update) | async-done | bytes 1835024 | tf_op jit(solution)/shard_map/all_gather | solution.py:168
  73.8 1353.7 %while.17 = (s32[]{:T(128)}, bf16[128,1024]{1,0:T(8,128)(2,1)S(1)}, f32[7,128]{1,0:T(8,128)S(1)}, s32[]{:T(128)}, pred[]{:T(512)}, /*index=5*/s32[7]{0:T(128)}, ...) while((s32[]{:T(128)}, bf16[128,1024]{1,0:T(8,128)(2,1)S(1)}, ...), condition=%wide.region_12.13_spmd.clone, body=%wide.region_0.12_spmd.clone.sunk | while | flops 944509184 | bytes 34627248 | solution.py:176
  88.3 10.1 collective-permute-start.2
  99.5 14.6 collective-permute-done.2
  114.0 10.6 conditional.7
  145.7 10.4 collective-permute-start.1
  166.4 26.2 %collective-permute-done.2 = f32[128,512]{1,0:T(8,128)S(1)} collective-permute-done((f32[128,512]{1,0:T(8,128)S(1)}, f32[128,512]{1,0:T(8,128)S(1)}, u32[]{:S(2)}, u32[]{:S(2)}) %collective-permute-start.2) | collective-permute-done | bytes 262176 | tf_op jit(solution)/shard_map/while/body/eval_jaxpr/ppermute | solution.py:23
  192.7 10.6 conditional.7
  233.1 18.3 %collective-permute-done.1 = f32[128,512]{0,1:T(8,128)} collective-permute-done((f32[128,512]{0,1:T(8,128)S(1)}, f32[128,512]{0,1:T(8,128)}, u32[]{:S(2)}, u32[]{:S(2)}) %collective-permute-start.1) | collective-permute-done | bytes 262176 | tf_op jit(solution)/shard_map/while/body/eval_jaxpr/ppermute | solution.py:17
  258.9 10.6 conditional.7
  301.0 11.5 collective-permute-done.1
  322.0 10.6 conditional.7
  364.6 11.5 collective-permute-done.1
  377.2 13.7 collective-permute-done.2
  391.0 10.6 conditional.7
  438.7 15.6 collective-permute-done.2
  454.3 10.6 conditional.7
  495.3 12.7 collective-permute-done.1
  509.1 9.7 collective-permute-done.2
  518.7 10.6 conditional.7
  556.1 18.5 %collective-permute-done.1 = f32[128,512]{0,1:T(8,128)} collective-permute-done((f32[128,512]{0,1:T(8,128)S(1)}, f32[128,512]{0,1:T(8,128)}, u32[]{:S(2)}, u32[]{:S(2)}) %collective-permute-start.1) | collective-permute-done | bytes 262176 | tf_op jit(solution)/shard_map/while/body/eval_jaxpr/ppermute | solution.py:17
  583.2 16.7 %collective-permute-start.3 = (bf16[128,1024]{1,0:T(8,128)(2,1)S(1)}, bf16[128,1024]{1,0:T(8,128)(2,1)S(1)}, u32[]{:S(2)}, u32[]{:S(2)}) collective-permute-start(bf16[128,1024]{1,0:T(8,128)(2,1)S(1)} %get-tuple-element.576), channel_id=1, source_target_pairs={{0,32},{32,64},{64,96},{96,128},{128,160},{160,192},{192,224},{224... | collective-permute-start | bytes 786440 | tf_op jit(solution)/shard_map/while/body/eval_jaxpr/ppermute | solution.py:17
  625.1 10.2 collective-permute-done
  636.7 12.2 collective-permute-done.2
  677.1 18.4 %collective-permute-done.1 = f32[128,512]{0,1:T(8,128)} collective-permute-done((f32[128,512]{0,1:T(8,128)S(1)}, f32[128,512]{0,1:T(8,128)}, u32[]{:S(2)}, u32[]{:S(2)}) %collective-permute-start.1) | collective-permute-done | bytes 262176 | tf_op jit(solution)/shard_map/while/body/eval_jaxpr/ppermute | solution.py:17
  704.1 17.6 %collective-permute-start.3 = (bf16[128,1024]{1,0:T(8,128)(2,1)S(1)}, bf16[128,1024]{1,0:T(8,128)(2,1)S(1)}, u32[]{:S(2)}, u32[]{:S(2)}) collective-permute-start(bf16[128,1024]{1,0:T(8,128)(2,1)S(1)} %get-tuple-element.576), channel_id=1, source_target_pairs={{0,32},{32,64},{64,96},{96,128},{128,160},{160,192},{192,224},{224... | collective-permute-start | bytes 786440 | tf_op jit(solution)/shard_map/while/body/eval_jaxpr/ppermute | solution.py:17
  744.8 12.1 collective-permute-done.1
  802.8 11.4 collective-permute-done.1
  822.3 18.7 %collective-permute-start.3 = (bf16[128,1024]{1,0:T(8,128)(2,1)S(1)}, bf16[128,1024]{1,0:T(8,128)(2,1)S(1)}, u32[]{:S(2)}, u32[]{:S(2)}) collective-permute-start(bf16[128,1024]{1,0:T(8,128)(2,1)S(1)} %get-tuple-element.576), channel_id=1, source_target_pairs={{0,32},{32,64},{64,96},{96,128},{128,160},{160,192},{192,224},{224... | collective-permute-start | bytes 786440 | tf_op jit(solution)/shard_map/while/body/eval_jaxpr/ppermute | solution.py:17
  865.9 15.8 %collective-permute-done.1 = f32[128,512]{0,1:T(8,128)} collective-permute-done((f32[128,512]{0,1:T(8,128)S(1)}, f32[128,512]{0,1:T(8,128)}, u32[]{:S(2)}, u32[]{:S(2)}) %collective-permute-start.1) | collective-permute-done | bytes 262176 | tf_op jit(solution)/shard_map/while/body/eval_jaxpr/ppermute | solution.py:17
  918.9 13.8 collective-permute-done
  943.1 16.5 %collective-permute-start.3 = (bf16[128,1024]{1,0:T(8,128)(2,1)S(1)}, bf16[128,1024]{1,0:T(8,128)(2,1)S(1)}, u32[]{:S(2)}, u32[]{:S(2)}) collective-permute-start(bf16[128,1024]{1,0:T(8,128)(2,1)S(1)} %get-tuple-element.576), channel_id=1, source_target_pairs={{0,32},{32,64},{64,96},{96,128},{128,160},{160,192},{192,224},{224... | collective-permute-start | bytes 786440 | tf_op jit(solution)/shard_map/while/body/eval_jaxpr/ppermute | solution.py:17
  983.6 11.4 collective-permute-done.1
  1004.8 10.5 collective-permute-start.3
  1037.5 13.8 collective-permute-done.1
  1060.0 15.9 %collective-permute-start.3 = (bf16[128,1024]{1,0:T(8,128)(2,1)S(1)}, bf16[128,1024]{1,0:T(8,128)(2,1)S(1)}, u32[]{:S(2)}, u32[]{:S(2)}) collective-permute-start(bf16[128,1024]{1,0:T(8,128)(2,1)S(1)} %get-tuple-element.576), channel_id=1, source_target_pairs={{0,32},{32,64},{64,96},{96,128},{128,160},{160,192},{192,224},{224... | collective-permute-start | bytes 786440 | tf_op jit(solution)/shard_map/while/body/eval_jaxpr/ppermute | solution.py:17
  1099.2 12.2 collective-permute-done.1
  1120.1 12.9 collective-permute-start.3
  1159.2 20.4 %collective-permute-done.2 = f32[128,512]{1,0:T(8,128)S(1)} collective-permute-done((f32[128,512]{1,0:T(8,128)S(1)}, f32[128,512]{1,0:T(8,128)S(1)}, u32[]{:S(2)}, u32[]{:S(2)}) %collective-permute-start.2) | collective-permute-done | bytes 262176 | tf_op jit(solution)/shard_map/while/body/eval_jaxpr/ppermute | solution.py:23
  1212.5 12.5 collective-permute-done.1
  1233.8 9.7 collective-permute-start.3
  1272.5 17.4 %collective-permute-done.1 = f32[128,512]{0,1:T(8,128)} collective-permute-done((f32[128,512]{0,1:T(8,128)S(1)}, f32[128,512]{0,1:T(8,128)}, u32[]{:S(2)}, u32[]{:S(2)}) %collective-permute-start.1) | collective-permute-done | bytes 262176 | tf_op jit(solution)/shard_map/while/body/eval_jaxpr/ppermute | solution.py:17
  1291.6 14.5 collective-permute-start.3
  1328.8 10.4 collective-permute-done
  1377.5 11.1 collective-permute-start.2
  1389.8 19.7 %collective-permute-done.2 = f32[128,512]{1,0:T(8,128)S(1)} collective-permute-done((f32[128,512]{1,0:T(8,128)S(1)}, f32[128,512]{1,0:T(8,128)S(1)}, u32[]{:S(2)}, u32[]{:S(2)}) %collective-permute-start.2) | collective-permute-done | bytes 262176 | tf_op jit(solution)/shard_map/while/body/eval_jaxpr/ppermute | solution.py:23
  1410.1 11.6 collective-permute-start.3
  1427.5 138.4 %all-reduce = f32[7,128]{1,0:T(8,128)S(1)} all-reduce(f32[7,128]{1,0:T(8,128)S(1)} %get-tuple-element.298), channel_id=2, replica_groups=mesh['section'=16,'tm'=32] {'section'}, use_global_device_ids=true, to_apply=%region_13.14.clone | all-reduce | flops 896 | bytes 7168
  (872 shorter events, 796.4 us)
Async XLA Ops:
  6.5 67.3 %all-gather.2.cloned.1.call-start = ((), (), s32[]{:S(2)}) async-start(), calls=%async_computation | async-start | bytes 1949696 | tf_op jit(solution)/shard_map/all_gather | solution.py:168
  88.3 25.8 %collective-permute-start.2 = (f32[128,512]{1,0:T(8,128)S(1)}, f32[128,512]{1,0:T(8,128)S(1)}, u32[]{:S(2)}, u32[]{:S(2)}) collective-permute-start(f32[128,512]{1,0:T(8,128)S(1)} %bitcast.72), channel_id=1, source_target_pairs={{0,16},{1,17},{2,18},{3,19},{4,20},{5,21},{6,22},{7,23},{8,24},{9,... | collective-permute-start | bytes 786440 | tf_op jit(solution)/shard_map/while/body/eval_jaxpr/ppermute | solution.py:23
  137.3 28.0 %collective-permute-start = (f32[128,512]{0,1:T(8,128)S(1)}, f32[128,512]{0,1:T(8,128)}, u32[]{:S(2)}, u32[]{:S(2)}) collective-permute-start(f32[128,512]{0,1:T(8,128)S(1)} %pad_maximum_fusion.8), channel_id=1, source_target_pairs={{0,1},{1,2},{2,3},{3,4},{4,5},{5,6},{6,7},{7,8},{8,9},{9,10},{10,1... | collective-permute-start | bytes 786440 | tf_op jit(solution)/shard_map/while/body/eval_jaxpr/ppermute | solution.py:17
  157.4 35.2 %collective-permute-start.2 = (f32[128,512]{1,0:T(8,128)S(1)}, f32[128,512]{1,0:T(8,128)S(1)}, u32[]{:S(2)}, u32[]{:S(2)}) collective-permute-start(f32[128,512]{1,0:T(8,128)S(1)} %bitcast.72), channel_id=1, source_target_pairs={{0,16},{1,17},{2,18},{3,19},{4,20},{5,21},{6,22},{7,23},{8,24},{9,... | collective-permute-start | bytes 786440 | tf_op jit(solution)/shard_map/while/body/eval_jaxpr/ppermute | solution.py:23
  223.0 28.4 %collective-permute-start.1 = (f32[128,512]{0,1:T(8,128)S(1)}, f32[128,512]{0,1:T(8,128)}, u32[]{:S(2)}, u32[]{:S(2)}) collective-permute-start(f32[128,512]{0,1:T(8,128)S(1)} %pad_maximum_fusion.8), channel_id=1, source_target_pairs={{0,2},{1,3},{2,4},{3,5},{4,6},{5,7},{6,8},{7,9},{8,10},{9,11},{10,... | collective-permute-start | bytes 786440 | tf_op jit(solution)/shard_map/while/body/eval_jaxpr/ppermute | solution.py:17
  226.2 32.7 %collective-permute-start.2 = (f32[128,512]{1,0:T(8,128)S(1)}, f32[128,512]{1,0:T(8,128)S(1)}, u32[]{:S(2)}, u32[]{:S(2)}) collective-permute-start(f32[128,512]{1,0:T(8,128)S(1)} %bitcast.72), channel_id=1, source_target_pairs={{0,16},{1,17},{2,18},{3,19},{4,20},{5,21},{6,22},{7,23},{8,24},{9,... | collective-permute-start | bytes 786440 | tf_op jit(solution)/shard_map/while/body/eval_jaxpr/ppermute | solution.py:23
  288.6 23.9 %collective-permute-start.1 = (f32[128,512]{0,1:T(8,128)S(1)}, f32[128,512]{0,1:T(8,128)}, u32[]{:S(2)}, u32[]{:S(2)}) collective-permute-start(f32[128,512]{0,1:T(8,128)S(1)} %pad_maximum_fusion.8), channel_id=1, source_target_pairs={{0,2},{1,3},{2,4},{3,5},{4,6},{5,7},{6,8},{7,9},{8,10},{9,11},{10,... | collective-permute-start | bytes 786440 | tf_op jit(solution)/shard_map/while/body/eval_jaxpr/ppermute | solution.py:17
  291.8 30.2 %collective-permute-start.2 = (f32[128,512]{1,0:T(8,128)S(1)}, f32[128,512]{1,0:T(8,128)S(1)}, u32[]{:S(2)}, u32[]{:S(2)}) collective-permute-start(f32[128,512]{1,0:T(8,128)S(1)} %bitcast.72), channel_id=1, source_target_pairs={{0,16},{1,17},{2,18},{3,19},{4,20},{5,21},{6,22},{7,23},{8,24},{9,... | collective-permute-start | bytes 786440 | tf_op jit(solution)/shard_map/while/body/eval_jaxpr/ppermute | solution.py:23
  353.4 22.8 %collective-permute-start.1 = (f32[128,512]{0,1:T(8,128)S(1)}, f32[128,512]{0,1:T(8,128)}, u32[]{:S(2)}, u32[]{:S(2)}) collective-permute-start(f32[128,512]{0,1:T(8,128)S(1)} %pad_maximum_fusion.8), channel_id=1, source_target_pairs={{0,2},{1,3},{2,4},{3,5},{4,6},{5,7},{6,8},{7,9},{8,10},{9,11},{10,... | collective-permute-start | bytes 786440 | tf_op jit(solution)/shard_map/while/body/eval_jaxpr/ppermute | solution.py:17
  356.6 34.4 %collective-permute-start.2 = (f32[128,512]{1,0:T(8,128)S(1)}, f32[128,512]{1,0:T(8,128)S(1)}, u32[]{:S(2)}, u32[]{:S(2)}) collective-permute-start(f32[128,512]{1,0:T(8,128)S(1)} %bitcast.72), channel_id=1, source_target_pairs={{0,16},{1,17},{2,18},{3,19},{4,20},{5,21},{6,22},{7,23},{8,24},{9,... | collective-permute-start | bytes 786440 | tf_op jit(solution)/shard_map/while/body/eval_jaxpr/ppermute | solution.py:23
  424.4 29.9 %collective-permute-start.2 = (f32[128,512]{1,0:T(8,128)S(1)}, f32[128,512]{1,0:T(8,128)S(1)}, u32[]{:S(2)}, u32[]{:S(2)}) collective-permute-start(f32[128,512]{1,0:T(8,128)S(1)} %bitcast.72), channel_id=1, source_target_pairs={{0,16},{1,17},{2,18},{3,19},{4,20},{5,21},{6,22},{7,23},{8,24},{9,... | collective-permute-start | bytes 786440 | tf_op jit(solution)/shard_map/while/body/eval_jaxpr/ppermute | solution.py:23
  485.3 22.7 %collective-permute-start.1 = (f32[128,512]{0,1:T(8,128)S(1)}, f32[128,512]{0,1:T(8,128)}, u32[]{:S(2)}, u32[]{:S(2)}) collective-permute-start(f32[128,512]{0,1:T(8,128)S(1)} %pad_maximum_fusion.8), channel_id=1, source_target_pairs={{0,2},{1,3},{2,4},{3,5},{4,6},{5,7},{6,8},{7,9},{8,10},{9,11},{10,... | collective-permute-start | bytes 786440 | tf_op jit(solution)/shard_map/while/body/eval_jaxpr/ppermute | solution.py:17
  488.5 30.2 %collective-permute-start.2 = (f32[128,512]{1,0:T(8,128)S(1)}, f32[128,512]{1,0:T(8,128)S(1)}, u32[]{:S(2)}, u32[]{:S(2)}) collective-permute-start(f32[128,512]{1,0:T(8,128)S(1)} %bitcast.72), channel_id=1, source_target_pairs={{0,16},{1,17},{2,18},{3,19},{4,20},{5,21},{6,22},{7,23},{8,24},{9,... | collective-permute-start | bytes 786440 | tf_op jit(solution)/shard_map/while/body/eval_jaxpr/ppermute | solution.py:23
  547.6 27.1 %collective-permute-start.1 = (f32[128,512]{0,1:T(8,128)S(1)}, f32[128,512]{0,1:T(8,128)}, u32[]{:S(2)}, u32[]{:S(2)}) collective-permute-start(f32[128,512]{0,1:T(8,128)S(1)} %pad_maximum_fusion.8), channel_id=1, source_target_pairs={{0,2},{1,3},{2,4},{3,5},{4,6},{5,7},{6,8},{7,9},{8,10},{9,11},{10,... | collective-permute-start | bytes 786440 | tf_op jit(solution)/shard_map/while/body/eval_jaxpr/ppermute | solution.py:17
  550.8 31.8 %collective-permute-start.2 = (f32[128,512]{1,0:T(8,128)S(1)}, f32[128,512]{1,0:T(8,128)S(1)}, u32[]{:S(2)}, u32[]{:S(2)}) collective-permute-start(f32[128,512]{1,0:T(8,128)S(1)} %bitcast.72), channel_id=1, source_target_pairs={{0,16},{1,17},{2,18},{3,19},{4,20},{5,21},{6,22},{7,23},{8,24},{9,... | collective-permute-start | bytes 786440 | tf_op jit(solution)/shard_map/while/body/eval_jaxpr/ppermute | solution.py:23
  583.2 22.5 %collective-permute-start.3 = (bf16[128,1024]{1,0:T(8,128)(2,1)S(1)}, bf16[128,1024]{1,0:T(8,128)(2,1)S(1)}, u32[]{:S(2)}, u32[]{:S(2)}) collective-permute-start(bf16[128,1024]{1,0:T(8,128)(2,1)S(1)} %get-tuple-element.576), channel_id=1, source_target_pairs={{0,32},{32,64},{64,96},{96,128},{128,160},{160,192},{192,224},{224... | collective-permute-start | bytes 786440 | tf_op jit(solution)/shard_map/while/body/eval_jaxpr/ppermute | solution.py:17
  610.7 24.7 %collective-permute-start = (f32[128,512]{0,1:T(8,128)S(1)}, f32[128,512]{0,1:T(8,128)}, u32[]{:S(2)}, u32[]{:S(2)}) collective-permute-start(f32[128,512]{0,1:T(8,128)S(1)} %pad_maximum_fusion.8), channel_id=1, source_target_pairs={{0,1},{1,2},{2,3},{3,4},{4,5},{5,6},{6,7},{7,8},{8,9},{9,10},{10,1... | collective-permute-start | bytes 786440 | tf_op jit(solution)/shard_map/while/body/eval_jaxpr/ppermute | solution.py:17
  612.7 22.9 %collective-permute-start.1 = (f32[128,512]{0,1:T(8,128)S(1)}, f32[128,512]{0,1:T(8,128)}, u32[]{:S(2)}, u32[]{:S(2)}) collective-permute-start(f32[128,512]{0,1:T(8,128)S(1)} %pad_maximum_fusion.8), channel_id=1, source_target_pairs={{0,2},{1,3},{2,4},{3,5},{4,6},{5,7},{6,8},{7,9},{8,10},{9,11},{10,... | collective-permute-start | bytes 786440 | tf_op jit(solution)/shard_map/while/body/eval_jaxpr/ppermute | solution.py:17
  615.9 32.9 %collective-permute-start.2 = (f32[128,512]{1,0:T(8,128)S(1)}, f32[128,512]{1,0:T(8,128)S(1)}, u32[]{:S(2)}, u32[]{:S(2)}) collective-permute-start(f32[128,512]{1,0:T(8,128)S(1)} %bitcast.72), channel_id=1, source_target_pairs={{0,16},{1,17},{2,18},{3,19},{4,20},{5,21},{6,22},{7,23},{8,24},{9,... | collective-permute-start | bytes 786440 | tf_op jit(solution)/shard_map/while/body/eval_jaxpr/ppermute | solution.py:23
  667.4 28.1 %collective-permute-start.1 = (f32[128,512]{0,1:T(8,128)S(1)}, f32[128,512]{0,1:T(8,128)}, u32[]{:S(2)}, u32[]{:S(2)}) collective-permute-start(f32[128,512]{0,1:T(8,128)S(1)} %pad_maximum_fusion.8), channel_id=1, source_target_pairs={{0,2},{1,3},{2,4},{3,5},{4,6},{5,7},{6,8},{7,9},{8,10},{9,11},{10,... | collective-permute-start | bytes 786440 | tf_op jit(solution)/shard_map/while/body/eval_jaxpr/ppermute | solution.py:17
  670.6 32.9 %collective-permute-start.2 = (f32[128,512]{1,0:T(8,128)S(1)}, f32[128,512]{1,0:T(8,128)S(1)}, u32[]{:S(2)}, u32[]{:S(2)}) collective-permute-start(f32[128,512]{1,0:T(8,128)S(1)} %bitcast.72), channel_id=1, source_target_pairs={{0,16},{1,17},{2,18},{3,19},{4,20},{5,21},{6,22},{7,23},{8,24},{9,... | collective-permute-start | bytes 786440 | tf_op jit(solution)/shard_map/while/body/eval_jaxpr/ppermute | solution.py:23
  704.1 23.3 %collective-permute-start.3 = (bf16[128,1024]{1,0:T(8,128)(2,1)S(1)}, bf16[128,1024]{1,0:T(8,128)(2,1)S(1)}, u32[]{:S(2)}, u32[]{:S(2)}) collective-permute-start(bf16[128,1024]{1,0:T(8,128)(2,1)S(1)} %get-tuple-element.576), channel_id=1, source_target_pairs={{0,32},{32,64},{64,96},{96,128},{128,160},{160,192},{192,224},{224... | collective-permute-start | bytes 786440 | tf_op jit(solution)/shard_map/while/body/eval_jaxpr/ppermute | solution.py:17
  734.4 22.5 %collective-permute-start.1 = (f32[128,512]{0,1:T(8,128)S(1)}, f32[128,512]{0,1:T(8,128)}, u32[]{:S(2)}, u32[]{:S(2)}) collective-permute-start(f32[128,512]{0,1:T(8,128)S(1)} %pad_maximum_fusion.8), channel_id=1, source_target_pairs={{0,2},{1,3},{2,4},{3,5},{4,6},{5,7},{6,8},{7,9},{8,10},{9,11},{10,... | collective-permute-start | bytes 786440 | tf_op jit(solution)/shard_map/while/body/eval_jaxpr/ppermute | solution.py:17
  737.6 28.1 %collective-permute-start.2 = (f32[128,512]{1,0:T(8,128)S(1)}, f32[128,512]{1,0:T(8,128)S(1)}, u32[]{:S(2)}, u32[]{:S(2)}) collective-permute-start(f32[128,512]{1,0:T(8,128)S(1)} %bitcast.72), channel_id=1, source_target_pairs={{0,16},{1,17},{2,18},{3,19},{4,20},{5,21},{6,22},{7,23},{8,24},{9,... | collective-permute-start | bytes 786440 | tf_op jit(solution)/shard_map/while/body/eval_jaxpr/ppermute | solution.py:23
  785.4 28.7 %collective-permute-start.1 = (f32[128,512]{0,1:T(8,128)S(1)}, f32[128,512]{0,1:T(8,128)}, u32[]{:S(2)}, u32[]{:S(2)}) collective-permute-start(f32[128,512]{0,1:T(8,128)S(1)} %pad_maximum_fusion.8), channel_id=1, source_target_pairs={{0,2},{1,3},{2,4},{3,5},{4,6},{5,7},{6,8},{7,9},{8,10},{9,11},{10,... | collective-permute-start | bytes 786440 | tf_op jit(solution)/shard_map/while/body/eval_jaxpr/ppermute | solution.py:17
  788.7 33.0 %collective-permute-start.2 = (f32[128,512]{1,0:T(8,128)S(1)}, f32[128,512]{1,0:T(8,128)S(1)}, u32[]{:S(2)}, u32[]{:S(2)}) collective-permute-start(f32[128,512]{1,0:T(8,128)S(1)} %bitcast.72), channel_id=1, source_target_pairs={{0,16},{1,17},{2,18},{3,19},{4,20},{5,21},{6,22},{7,23},{8,24},{9,... | collective-permute-start | bytes 786440 | tf_op jit(solution)/shard_map/while/body/eval_jaxpr/ppermute | solution.py:23
  822.3 24.4 %collective-permute-start.3 = (bf16[128,1024]{1,0:T(8,128)(2,1)S(1)}, bf16[128,1024]{1,0:T(8,128)(2,1)S(1)}, u32[]{:S(2)}, u32[]{:S(2)}) collective-permute-start(bf16[128,1024]{1,0:T(8,128)(2,1)S(1)} %get-tuple-element.576), channel_id=1, source_target_pairs={{0,32},{32,64},{64,96},{96,128},{128,160},{160,192},{192,224},{224... | collective-permute-start | bytes 786440 | tf_op jit(solution)/shard_map/while/body/eval_jaxpr/ppermute | solution.py:17
  853.6 28.1 %collective-permute-start.1 = (f32[128,512]{0,1:T(8,128)S(1)}, f32[128,512]{0,1:T(8,128)}, u32[]{:S(2)}, u32[]{:S(2)}) collective-permute-start(f32[128,512]{0,1:T(8,128)S(1)} %pad_maximum_fusion.8), channel_id=1, source_target_pairs={{0,2},{1,3},{2,4},{3,5},{4,6},{5,7},{6,8},{7,9},{8,10},{9,11},{10,... | collective-permute-start | bytes 786440 | tf_op jit(solution)/shard_map/while/body/eval_jaxpr/ppermute | solution.py:17
  856.8 35.0 %collective-permute-start.2 = (f32[128,512]{1,0:T(8,128)S(1)}, f32[128,512]{1,0:T(8,128)S(1)}, u32[]{:S(2)}, u32[]{:S(2)}) collective-permute-start(f32[128,512]{1,0:T(8,128)S(1)} %bitcast.72), channel_id=1, source_target_pairs={{0,16},{1,17},{2,18},{3,19},{4,20},{5,21},{6,22},{7,23},{8,24},{9,... | collective-permute-start | bytes 786440 | tf_op jit(solution)/shard_map/while/body/eval_jaxpr/ppermute | solution.py:23
  907.1 25.5 %collective-permute-start = (f32[128,512]{0,1:T(8,128)S(1)}, f32[128,512]{0,1:T(8,128)}, u32[]{:S(2)}, u32[]{:S(2)}) collective-permute-start(f32[128,512]{0,1:T(8,128)S(1)} %pad_maximum_fusion.8), channel_id=1, source_target_pairs={{0,1},{1,2},{2,3},{3,4},{4,5},{5,6},{6,7},{7,8},{8,9},{9,10},{10,1... | collective-permute-start | bytes 786440 | tf_op jit(solution)/shard_map/while/body/eval_jaxpr/ppermute | solution.py:17
  909.2 25.3 %collective-permute-start.1 = (f32[128,512]{0,1:T(8,128)S(1)}, f32[128,512]{0,1:T(8,128)}, u32[]{:S(2)}, u32[]{:S(2)}) collective-permute-start(f32[128,512]{0,1:T(8,128)S(1)} %pad_maximum_fusion.8), channel_id=1, source_target_pairs={{0,2},{1,3},{2,4},{3,5},{4,6},{5,7},{6,8},{7,9},{8,10},{9,11},{10,... | collective-permute-start | bytes 786440 | tf_op jit(solution)/shard_map/while/body/eval_jaxpr/ppermute | solution.py:17
  912.4 30.2 %collective-permute-start.2 = (f32[128,512]{1,0:T(8,128)S(1)}, f32[128,512]{1,0:T(8,128)S(1)}, u32[]{:S(2)}, u32[]{:S(2)}) collective-permute-start(f32[128,512]{1,0:T(8,128)S(1)} %bitcast.72), channel_id=1, source_target_pairs={{0,16},{1,17},{2,18},{3,19},{4,20},{5,21},{6,22},{7,23},{8,24},{9,... | collective-permute-start | bytes 786440 | tf_op jit(solution)/shard_map/while/body/eval_jaxpr/ppermute | solution.py:23
  943.1 22.4 %collective-permute-start.3 = (bf16[128,1024]{1,0:T(8,128)(2,1)S(1)}, bf16[128,1024]{1,0:T(8,128)(2,1)S(1)}, u32[]{:S(2)}, u32[]{:S(2)}) collective-permute-start(bf16[128,1024]{1,0:T(8,128)(2,1)S(1)} %get-tuple-element.576), channel_id=1, source_target_pairs={{0,32},{32,64},{64,96},{96,128},{128,160},{160,192},{192,224},{224... | collective-permute-start | bytes 786440 | tf_op jit(solution)/shard_map/while/body/eval_jaxpr/ppermute | solution.py:17
  972.5 22.5 %collective-permute-start.1 = (f32[128,512]{0,1:T(8,128)S(1)}, f32[128,512]{0,1:T(8,128)}, u32[]{:S(2)}, u32[]{:S(2)}) collective-permute-start(f32[128,512]{0,1:T(8,128)S(1)} %pad_maximum_fusion.8), channel_id=1, source_target_pairs={{0,2},{1,3},{2,4},{3,5},{4,6},{5,7},{6,8},{7,9},{8,10},{9,11},{10,... | collective-permute-start | bytes 786440 | tf_op jit(solution)/shard_map/while/body/eval_jaxpr/ppermute | solution.py:17
  975.7 28.5 %collective-permute-start.2 = (f32[128,512]{1,0:T(8,128)S(1)}, f32[128,512]{1,0:T(8,128)S(1)}, u32[]{:S(2)}, u32[]{:S(2)}) collective-permute-start(f32[128,512]{1,0:T(8,128)S(1)} %bitcast.72), channel_id=1, source_target_pairs={{0,16},{1,17},{2,18},{3,19},{4,20},{5,21},{6,22},{7,23},{8,24},{9,... | collective-permute-start | bytes 786440 | tf_op jit(solution)/shard_map/while/body/eval_jaxpr/ppermute | solution.py:23
  1028.2 23.1 %collective-permute-start.1 = (f32[128,512]{0,1:T(8,128)S(1)}, f32[128,512]{0,1:T(8,128)}, u32[]{:S(2)}, u32[]{:S(2)}) collective-permute-start(f32[128,512]{0,1:T(8,128)S(1)} %pad_maximum_fusion.8), channel_id=1, source_target_pairs={{0,2},{1,3},{2,4},{3,5},{4,6},{5,7},{6,8},{7,9},{8,10},{9,11},{10,... | collective-permute-start | bytes 786440 | tf_op jit(solution)/shard_map/while/body/eval_jaxpr/ppermute | solution.py:17
  1031.4 27.9 %collective-permute-start.2 = (f32[128,512]{1,0:T(8,128)S(1)}, f32[128,512]{1,0:T(8,128)S(1)}, u32[]{:S(2)}, u32[]{:S(2)}) collective-permute-start(f32[128,512]{1,0:T(8,128)S(1)} %bitcast.72), channel_id=1, source_target_pairs={{0,16},{1,17},{2,18},{3,19},{4,20},{5,21},{6,22},{7,23},{8,24},{9,... | collective-permute-start | bytes 786440 | tf_op jit(solution)/shard_map/while/body/eval_jaxpr/ppermute | solution.py:23
  1060.0 21.9 %collective-permute-start.3 = (bf16[128,1024]{1,0:T(8,128)(2,1)S(1)}, bf16[128,1024]{1,0:T(8,128)(2,1)S(1)}, u32[]{:S(2)}, u32[]{:S(2)}) collective-permute-start(bf16[128,1024]{1,0:T(8,128)(2,1)S(1)} %get-tuple-element.576), channel_id=1, source_target_pairs={{0,32},{32,64},{64,96},{96,128},{128,160},{160,192},{192,224},{224... | collective-permute-start | bytes 786440 | tf_op jit(solution)/shard_map/while/body/eval_jaxpr/ppermute | solution.py:17
  1089.7 21.7 %collective-permute-start.1 = (f32[128,512]{0,1:T(8,128)S(1)}, f32[128,512]{0,1:T(8,128)}, u32[]{:S(2)}, u32[]{:S(2)}) collective-permute-start(f32[128,512]{0,1:T(8,128)S(1)} %pad_maximum_fusion.8), channel_id=1, source_target_pairs={{0,2},{1,3},{2,4},{3,5},{4,6},{5,7},{6,8},{7,9},{8,10},{9,11},{10,... | collective-permute-start | bytes 786440 | tf_op jit(solution)/shard_map/while/body/eval_jaxpr/ppermute | solution.py:17
  1092.9 26.6 %collective-permute-start.2 = (f32[128,512]{1,0:T(8,128)S(1)}, f32[128,512]{1,0:T(8,128)S(1)}, u32[]{:S(2)}, u32[]{:S(2)}) collective-permute-start(f32[128,512]{1,0:T(8,128)S(1)} %bitcast.72), channel_id=1, source_target_pairs={{0,16},{1,17},{2,18},{3,19},{4,20},{5,21},{6,22},{7,23},{8,24},{9,... | collective-permute-start | bytes 786440 | tf_op jit(solution)/shard_map/while/body/eval_jaxpr/ppermute | solution.py:23
  1148.7 30.9 %collective-permute-start.2 = (f32[128,512]{1,0:T(8,128)S(1)}, f32[128,512]{1,0:T(8,128)S(1)}, u32[]{:S(2)}, u32[]{:S(2)}) collective-permute-start(f32[128,512]{1,0:T(8,128)S(1)} %bitcast.72), channel_id=1, source_target_pairs={{0,16},{1,17},{2,18},{3,19},{4,20},{5,21},{6,22},{7,23},{8,24},{9,... | collective-permute-start | bytes 786440 | tf_op jit(solution)/shard_map/while/body/eval_jaxpr/ppermute | solution.py:23
  1206.7 26.5 %collective-permute-start.2 = (f32[128,512]{1,0:T(8,128)S(1)}, f32[128,512]{1,0:T(8,128)S(1)}, u32[]{:S(2)}, u32[]{:S(2)}) collective-permute-start(f32[128,512]{1,0:T(8,128)S(1)} %bitcast.72), channel_id=1, source_target_pairs={{0,16},{1,17},{2,18},{3,19},{4,20},{5,21},{6,22},{7,23},{8,24},{9,... | collective-permute-start | bytes 786440 | tf_op jit(solution)/shard_map/while/body/eval_jaxpr/ppermute | solution.py:23
  1256.2 33.6 %collective-permute-start.1 = (f32[128,512]{0,1:T(8,128)S(1)}, f32[128,512]{0,1:T(8,128)}, u32[]{:S(2)}, u32[]{:S(2)}) collective-permute-start(f32[128,512]{0,1:T(8,128)S(1)} %pad_maximum_fusion.8), channel_id=1, source_target_pairs={{0,2},{1,3},{2,4},{3,5},{4,6},{5,7},{6,8},{7,9},{8,10},{9,11},{10,... | collective-permute-start | bytes 786440 | tf_op jit(solution)/shard_map/while/body/eval_jaxpr/ppermute | solution.py:17
  1259.4 31.6 %collective-permute-start.2 = (f32[128,512]{1,0:T(8,128)S(1)}, f32[128,512]{1,0:T(8,128)S(1)}, u32[]{:S(2)}, u32[]{:S(2)}) collective-permute-start(f32[128,512]{1,0:T(8,128)S(1)} %bitcast.72), channel_id=1, source_target_pairs={{0,16},{1,17},{2,18},{3,19},{4,20},{5,21},{6,22},{7,23},{8,24},{9,... | collective-permute-start | bytes 786440 | tf_op jit(solution)/shard_map/while/body/eval_jaxpr/ppermute | solution.py:23
  1317.3 22.0 %collective-permute-start = (f32[128,512]{0,1:T(8,128)S(1)}, f32[128,512]{0,1:T(8,128)}, u32[]{:S(2)}, u32[]{:S(2)}) collective-permute-start(f32[128,512]{0,1:T(8,128)S(1)} %pad_maximum_fusion.8), channel_id=1, source_target_pairs={{0,1},{1,2},{2,3},{3,4},{4,5},{5,6},{6,7},{7,8},{8,9},{9,10},{10,1... | collective-permute-start | bytes 786440 | tf_op jit(solution)/shard_map/while/body/eval_jaxpr/ppermute | solution.py:17
  1319.3 26.2 %collective-permute-start.1 = (f32[128,512]{0,1:T(8,128)S(1)}, f32[128,512]{0,1:T(8,128)}, u32[]{:S(2)}, u32[]{:S(2)}) collective-permute-start(f32[128,512]{0,1:T(8,128)S(1)} %pad_maximum_fusion.8), channel_id=1, source_target_pairs={{0,2},{1,3},{2,4},{3,5},{4,6},{5,7},{6,8},{7,9},{8,10},{9,11},{10,... | collective-permute-start | bytes 786440 | tf_op jit(solution)/shard_map/while/body/eval_jaxpr/ppermute | solution.py:17
  1322.5 31.6 %collective-permute-start.2 = (f32[128,512]{1,0:T(8,128)S(1)}, f32[128,512]{1,0:T(8,128)S(1)}, u32[]{:S(2)}, u32[]{:S(2)}) collective-permute-start(f32[128,512]{1,0:T(8,128)S(1)} %bitcast.72), channel_id=1, source_target_pairs={{0,16},{1,17},{2,18},{3,19},{4,20},{5,21},{6,22},{7,23},{8,24},{9,... | collective-permute-start | bytes 786440 | tf_op jit(solution)/shard_map/while/body/eval_jaxpr/ppermute | solution.py:23
  1377.5 32.0 %collective-permute-start.2 = (f32[128,512]{1,0:T(8,128)S(1)}, f32[128,512]{1,0:T(8,128)S(1)}, u32[]{:S(2)}, u32[]{:S(2)}) collective-permute-start(f32[128,512]{1,0:T(8,128)S(1)} %bitcast.72), channel_id=1, source_target_pairs={{0,16},{1,17},{2,18},{3,19},{4,20},{5,21},{6,22},{7,23},{8,24},{9,... | collective-permute-start | bytes 786440 | tf_op jit(solution)/shard_map/while/body/eval_jaxpr/ppermute | solution.py:23
  (99 other events, 2271.7 us)
Sparse Core Ops, SparseCore 0:
  10.4 63.3 all-gather.1
where the time goes:
time: 1580 us; the launch traced here: 1570 us
  waiting for transfers between devices  664 us (42%)
  starting transfers between devices  473 us (30%)
  blocking collectives  138 us (9%)
  local copies, waits for them, and re-layouts  107 us (7%)
  other arithmetic  79 us (5%)
  loops' own time  50.8 us (3%)
  matrix products  47.2 us (3%)
    ppermute x66, waiting for transfers between devices, from_behind(): lax.ppermute(value, axis, [(source, source + steps) for source in range(l...  372 us
    ppermute x66, starting transfers between devices, from_behind(): lax.ppermute(value, axis, [(source, source + steps) for source in range(l...  314 us
    ppermute x22, waiting for transfers between devices, passed_along(): return lax.ppermute(value, axis, pairs)  228 us
    ppermute x22, starting transfers between devices, passed_along(): return lax.ppermute(value, axis, pairs)  159 us
    unnamed x1, blocking collectives  138 us
    all_gather x1, waiting for transfers between devices, local(): whole_series = lax.all_gather(series, 'section', axis=2, tiled=True)  62.6 us
    another operation x1, loops' own time, local(): final_state, totals = lax.fori_loop(0, tick_count, tick_all, initial)  49 us
  transfers between devices with their start and end apart: 89, of which 72 were waited for; matrix products, arithmetic and copies ran while one was open for 5% of the time, Pallas kernels for 0%

commit v1 on v0

--- a/solution.py
+++ b/solution.py
@@ -165,7 +165,14 @@
         jnp.zeros((row_count, model_width), jnp.bfloat16),
         jnp.zeros((micro_count, row_count), jnp.float32),
     )
-    whole_series = lax.all_gather(series, "section", axis=2, tiled=True)
+    ring = [series]
+    for hop in range(15):
+        ring.append(lax.ppermute(ring[-1], "section", [(dev, (dev + 1) % 16) for dev in range(16)]))
+    whole_series = jnp.roll(
+        jnp.concatenate(ring[::-1], axis=2),
+        (lax.axis_index("section") + 1) * ring[0].shape[2],
+        axis=2,
+    )
 
     def tick_all(tick_index, carry):
         slot_here = jnp.clip(tick_index, 0, micro_count - 1)

time: 1580 us -> 1680 us (1.063)
  the two profiles are of different devices: /device:TPU:64 before, /device:TPU:128 now
where the time goes in v1:
time: 1680 us
  waiting for transfers between devices  633 us (38%)
  starting transfers between devices  604 us (36%)
  blocking collectives  157 us (9%)
  other arithmetic  102 us (6%)
  local copies, waits for them, and re-layouts  92.4 us (6%)
  loops' own time  46.5 us (3%)
  matrix products  39.9 us (2%)
    ppermute x66, starting transfers between devices, from_behind(): lax.ppermute(value, axis, [(source, source + steps) for source in range(l...  426 us
    ppermute x22, waiting for transfers between devices, passed_along(): return lax.ppermute(value, axis, pairs)  284 us
    ppermute x66, waiting for transfers between devices, from_behind(): lax.ppermute(value, axis, [(source, source + steps) for source in range(l...  207 us
    unnamed x1, blocking collectives  157 us
    ppermute x22, starting transfers between devices, passed_along(): return lax.ppermute(value, axis, pairs)  147 us
    ppermute x15, waiting for transfers between devices, local(): lax.ppermute(ring[-1], 'section', [(dev, (dev + 1) % 16) for dev in range...  142 us
    another operation x1, loops' own time, local(): final_state, totals = lax.fori_loop(0, tick_count, tick_all, initial)  44.7 us
  transfers between devices with their start and end apart: 103, of which 79 were waited for; matrix products, arithmetic and copies ran while one was open for 4% of the time, Pallas kernels for 0%

profile of v1, /device:TPU:128, one launch (start us, length us, event | category | flops | bytes accessed | tf_op | source)
XLA Modules:
  0.0 1675.5 jit_solution(15677089550850609470)
XLA Ops:
  15.7 9.9 collective-permute-done.5
  83.7 10.1 collective-permute-done.11
  95.7 11.3 collective-permute-done.12
  109.0 11.0 collective-permute-done.13
  121.9 10.2 collective-permute-done.14
  177.5 12.6 concatenate.46
  193.9 1323.9 %while.17 = (s32[]{:T(128)}, bf16[128,1024]{1,0:T(8,128)(2,1)S(1)}, f32[7,128]{1,0:T(8,128)S(1)}, s32[]{:T(128)}, pred[]{:T(512)}, /*index=5*/s32[7]{0:T(128)}, ...) while((s32[]{:T(128)}, bf16[128,1024]{1,0:T(8,128)(2,1)S(1)}, ...), condition=%wide.region_12.13_spmd.clone, body=%wide.region_0.12_spmd.clone.sunk | while | flops 944509184 | bytes 31460984 | solution.py:183
  208.1 10.0 collective-permute-start.2
  219.1 14.2 collective-permute-done.2
  265.7 12.2 collective-permute-start.2
  285.2 9.4 conditional.7
  315.1 25.1 %collective-permute-start.1 = (f32[128,512]{0,1:T(8,128)S(1)}, f32[128,512]{0,1:T(8,128)}, u32[]{:S(2)}, u32[]{:S(2)}) collective-permute-start(f32[128,512]{0,1:T(8,128)S(1)} %pad_maximum_fusion.8), channel_id=1, source_target_pairs={{0,2},{1,3},{2,4},{3,5},{4,6},{5,7},{6,8},{7,9},{8,10},{9,11},{10,... | collective-permute-start | bytes 786440 | tf_op jit(solution)/shard_map/while/body/eval_jaxpr/ppermute | solution.py:17
  348.0 22.7 %collective-permute-done.2 = f32[128,512]{1,0:T(8,128)S(1)} collective-permute-done((f32[128,512]{1,0:T(8,128)S(1)}, f32[128,512]{1,0:T(8,128)S(1)}, u32[]{:S(2)}, u32[]{:S(2)}) %collective-permute-start.2) | collective-permute-done | bytes 262176 | tf_op jit(solution)/shard_map/while/body/eval_jaxpr/ppermute | solution.py:23
  370.6 9.4 conditional.7
  412.7 20.0 %collective-permute-done.2 = f32[128,512]{1,0:T(8,128)S(1)} collective-permute-done((f32[128,512]{1,0:T(8,128)S(1)}, f32[128,512]{1,0:T(8,128)S(1)}, u32[]{:S(2)}, u32[]{:S(2)}) %collective-permute-start.2) | collective-permute-done | bytes 262176 | tf_op jit(solution)/shard_map/while/body/eval_jaxpr/ppermute | solution.py:23
  432.7 9.4 conditional.7
  475.8 14.0 collective-permute-done.1
  497.5 9.4 conditional.7
  530.9 10.1 collective-permute-start.2
  547.6 11.8 collective-permute-done.2
  559.4 9.4 conditional.7
  613.4 11.5 collective-permute-done.2
  624.9 9.4 conditional.7
  665.0 10.4 collective-permute-done.1
  685.2 16.1 collective-permute-start.3
  737.7 10.5 collective-permute-start.3
  782.5 21.5 %collective-permute-done.2 = f32[128,512]{1,0:T(8,128)S(1)} collective-permute-done((f32[128,512]{1,0:T(8,128)S(1)}, f32[128,512]{1,0:T(8,128)S(1)}, u32[]{:S(2)}, u32[]{:S(2)}) %collective-permute-start.2) | collective-permute-done | bytes 262176 | tf_op jit(solution)/shard_map/while/body/eval_jaxpr/ppermute | solution.py:23
  804.5 18.8 %collective-permute-start.3 = (bf16[128,1024]{1,0:T(8,128)(2,1)S(1)}, bf16[128,1024]{1,0:T(8,128)(2,1)S(1)}, u32[]{:S(2)}, u32[]{:S(2)}) collective-permute-start(bf16[128,1024]{1,0:T(8,128)(2,1)S(1)} %get-tuple-element.560), channel_id=1, source_target_pairs={{0,32},{32,64},{64,96},{96,128},{128,160},{160,192},{192,224},{224... | collective-permute-start | bytes 786440 | tf_op jit(solution)/shard_map/while/body/eval_jaxpr/ppermute | solution.py:17
  851.5 16.5 collective-permute-done.2
  868.5 11.6 collective-permute-start.3
  904.2 9.5 collective-permute-done.1
  914.7 11.9 collective-permute-done.2
  947.8 14.9 collective-permute-start.1
  973.7 18.9 %collective-permute-done.2 = f32[128,512]{1,0:T(8,128)S(1)} collective-permute-done((f32[128,512]{1,0:T(8,128)S(1)}, f32[128,512]{1,0:T(8,128)S(1)}, u32[]{:S(2)}, u32[]{:S(2)}) %collective-permute-start.2) | collective-permute-done | bytes 262176 | tf_op jit(solution)/shard_map/while/body/eval_jaxpr/ppermute | solution.py:23
  1027.0 13.4 collective-permute-done.2
  1041.0 18.6 %collective-permute-start.3 = (bf16[128,1024]{1,0:T(8,128)(2,1)S(1)}, bf16[128,1024]{1,0:T(8,128)(2,1)S(1)}, u32[]{:S(2)}, u32[]{:S(2)}) collective-permute-start(bf16[128,1024]{1,0:T(8,128)(2,1)S(1)} %get-tuple-element.560), channel_id=1, source_target_pairs={{0,32},{32,64},{64,96},{96,128},{128,160},{160,192},{192,224},{224... | collective-permute-start | bytes 786440 | tf_op jit(solution)/shard_map/while/body/eval_jaxpr/ppermute | solution.py:17
  1090.1 23.3 %collective-permute-done.2 = f32[128,512]{1,0:T(8,128)S(1)} collective-permute-done((f32[128,512]{1,0:T(8,128)S(1)}, f32[128,512]{1,0:T(8,128)S(1)}, u32[]{:S(2)}, u32[]{:S(2)}) %collective-permute-start.2) | collective-permute-done | bytes 262176 | tf_op jit(solution)/shard_map/while/body/eval_jaxpr/ppermute | solution.py:23
  1148.2 18.3 %collective-permute-done.2 = f32[128,512]{1,0:T(8,128)S(1)} collective-permute-done((f32[128,512]{1,0:T(8,128)S(1)}, f32[128,512]{1,0:T(8,128)S(1)}, u32[]{:S(2)}, u32[]{:S(2)}) %collective-permute-start.2) | collective-permute-done | bytes 262176 | tf_op jit(solution)/shard_map/while/body/eval_jaxpr/ppermute | solution.py:23
  1183.9 10.6 collective-permute-start
  1209.9 14.2 collective-permute-done.2
  1270.8 17.6 %collective-permute-start.3 = (bf16[128,1024]{1,0:T(8,128)(2,1)S(1)}, bf16[128,1024]{1,0:T(8,128)(2,1)S(1)}, u32[]{:S(2)}, u32[]{:S(2)}) collective-permute-start(bf16[128,1024]{1,0:T(8,128)(2,1)S(1)} %get-tuple-element.560), channel_id=1, source_target_pairs={{0,32},{32,64},{64,96},{96,128},{128,160},{160,192},{192,224},{224... | collective-permute-start | bytes 786440 | tf_op jit(solution)/shard_map/while/body/eval_jaxpr/ppermute | solution.py:17
  1341.3 14.0 collective-permute-start
  1355.3 11.5 collective-permute-start.1
  1373.9 10.8 collective-permute-done.1
  1395.5 18.5 %collective-permute-start.3 = (bf16[128,1024]{1,0:T(8,128)(2,1)S(1)}, bf16[128,1024]{1,0:T(8,128)(2,1)S(1)}, u32[]{:S(2)}, u32[]{:S(2)}) collective-permute-start(bf16[128,1024]{1,0:T(8,128)(2,1)S(1)} %get-tuple-element.560), channel_id=1, source_target_pairs={{0,32},{32,64},{64,96},{96,128},{128,160},{160,192},{192,224},{224... | collective-permute-start | bytes 786440 | tf_op jit(solution)/shard_map/while/body/eval_jaxpr/ppermute | solution.py:17
  1487.7 10.7 collective-permute-done.2
  1498.9 15.0 collective-permute-start.3
  1517.7 157.1 %all-reduce = f32[7,128]{1,0:T(8,128)S(1)} all-reduce(f32[7,128]{1,0:T(8,128)S(1)} %get-tuple-element.298), channel_id=2, replica_groups=mesh['section'=16,'tm'=32] {'section'}, use_global_device_ids=true, to_apply=%region_13.14.clone | all-reduce | flops 896 | bytes 7168
  (776 shorter events, 934.9 us)
Async XLA Ops:
  208.1 25.3 %collective-permute-start.2 = (f32[128,512]{1,0:T(8,128)S(1)}, f32[128,512]{1,0:T(8,128)S(1)}, u32[]{:S(2)}, u32[]{:S(2)}) collective-permute-start(f32[128,512]{1,0:T(8,128)S(1)} %bitcast.72), channel_id=1, source_target_pairs={{0,16},{1,17},{2,18},{3,19},{4,20},{5,21},{6,22},{7,23},{8,24},{9,... | collective-permute-start | bytes 786440 | tf_op jit(solution)/shard_map/while/body/eval_jaxpr/ppermute | solution.py:23
  257.7 20.3 %collective-permute-start = (f32[128,512]{0,1:T(8,128)S(1)}, f32[128,512]{0,1:T(8,128)S(1)}, u32[]{:S(2)}, u32[]{:S(2)}) collective-permute-start(f32[128,512]{0,1:T(8,128)S(1)} %pad_maximum_fusion.8), channel_id=1, source_target_pairs={{0,1},{1,2},{2,3},{3,4},{4,5},{5,6},{6,7},{7,8},{8,9},{9,10},{10,1... | collective-permute-start | bytes 786440 | tf_op jit(solution)/shard_map/while/body/eval_jaxpr/ppermute | solution.py:17
  259.6 18.4 %collective-permute-start.1 = (f32[128,512]{0,1:T(8,128)S(1)}, f32[128,512]{0,1:T(8,128)}, u32[]{:S(2)}, u32[]{:S(2)}) collective-permute-start(f32[128,512]{0,1:T(8,128)S(1)} %pad_maximum_fusion.8), channel_id=1, source_target_pairs={{0,2},{1,3},{2,4},{3,5},{4,6},{5,7},{6,8},{7,9},{8,10},{9,11},{10,... | collective-permute-start | bytes 786440 | tf_op jit(solution)/shard_map/while/body/eval_jaxpr/ppermute | solution.py:17
  265.7 19.4 %collective-permute-start.2 = (f32[128,512]{1,0:T(8,128)S(1)}, f32[128,512]{1,0:T(8,128)S(1)}, u32[]{:S(2)}, u32[]{:S(2)}) collective-permute-start(f32[128,512]{1,0:T(8,128)S(1)} %bitcast.72), channel_id=1, source_target_pairs={{0,16},{1,17},{2,18},{3,19},{4,20},{5,21},{6,22},{7,23},{8,24},{9,... | collective-permute-start | bytes 786440 | tf_op jit(solution)/shard_map/while/body/eval_jaxpr/ppermute | solution.py:23
  310.0 34.5 %collective-permute-start = (f32[128,512]{0,1:T(8,128)S(1)}, f32[128,512]{0,1:T(8,128)S(1)}, u32[]{:S(2)}, u32[]{:S(2)}) collective-permute-start(f32[128,512]{0,1:T(8,128)S(1)} %pad_maximum_fusion.8), channel_id=1, source_target_pairs={{0,1},{1,2},{2,3},{3,4},{4,5},{5,6},{6,7},{7,8},{8,9},{9,10},{10,1... | collective-permute-start | bytes 786440 | tf_op jit(solution)/shard_map/while/body/eval_jaxpr/ppermute | solution.py:17
  315.1 31.8 %collective-permute-start.1 = (f32[128,512]{0,1:T(8,128)S(1)}, f32[128,512]{0,1:T(8,128)}, u32[]{:S(2)}, u32[]{:S(2)}) collective-permute-start(f32[128,512]{0,1:T(8,128)S(1)} %pad_maximum_fusion.8), channel_id=1, source_target_pairs={{0,2},{1,3},{2,4},{3,5},{4,6},{5,7},{6,8},{7,9},{8,10},{9,11},{10,... | collective-permute-start | bytes 786440 | tf_op jit(solution)/shard_map/while/body/eval_jaxpr/ppermute | solution.py:17
  341.5 29.1 %collective-permute-start.2 = (f32[128,512]{1,0:T(8,128)S(1)}, f32[128,512]{1,0:T(8,128)S(1)}, u32[]{:S(2)}, u32[]{:S(2)}) collective-permute-start(f32[128,512]{1,0:T(8,128)S(1)} %bitcast.72), channel_id=1, source_target_pairs={{0,16},{1,17},{2,18},{3,19},{4,20},{5,21},{6,22},{7,23},{8,24},{9,... | collective-permute-start | bytes 786440 | tf_op jit(solution)/shard_map/while/body/eval_jaxpr/ppermute | solution.py:23
  403.1 29.6 %collective-permute-start.2 = (f32[128,512]{1,0:T(8,128)S(1)}, f32[128,512]{1,0:T(8,128)S(1)}, u32[]{:S(2)}, u32[]{:S(2)}) collective-permute-start(f32[128,512]{1,0:T(8,128)S(1)} %bitcast.72), channel_id=1, source_target_pairs={{0,16},{1,17},{2,18},{3,19},{4,20},{5,21},{6,22},{7,23},{8,24},{9,... | collective-permute-start | bytes 786440 | tf_op jit(solution)/shard_map/while/body/eval_jaxpr/ppermute | solution.py:23
  462.8 27.1 %collective-permute-start.1 = (f32[128,512]{0,1:T(8,128)S(1)}, f32[128,512]{0,1:T(8,128)}, u32[]{:S(2)}, u32[]{:S(2)}) collective-permute-start(f32[128,512]{0,1:T(8,128)S(1)} %pad_maximum_fusion.8), channel_id=1, source_target_pairs={{0,2},{1,3},{2,4},{3,5},{4,6},{5,7},{6,8},{7,9},{8,10},{9,11},{10,... | collective-permute-start | bytes 786440 | tf_op jit(solution)/shard_map/while/body/eval_jaxpr/ppermute | solution.py:17
  472.7 24.8 %collective-permute-start.2 = (f32[128,512]{1,0:T(8,128)S(1)}, f32[128,512]{1,0:T(8,128)S(1)}, u32[]{:S(2)}, u32[]{:S(2)}) collective-permute-start(f32[128,512]{1,0:T(8,128)S(1)} %bitcast.72), channel_id=1, source_target_pairs={{0,16},{1,17},{2,18},{3,19},{4,20},{5,21},{6,22},{7,23},{8,24},{9,... | collective-permute-start | bytes 786440 | tf_op jit(solution)/shard_map/while/body/eval_jaxpr/ppermute | solution.py:23
  526.8 19.8 %collective-permute-start.1 = (f32[128,512]{0,1:T(8,128)S(1)}, f32[128,512]{0,1:T(8,128)}, u32[]{:S(2)}, u32[]{:S(2)}) collective-permute-start(f32[128,512]{0,1:T(8,128)S(1)} %pad_maximum_fusion.8), channel_id=1, source_target_pairs={{0,2},{1,3},{2,4},{3,5},{4,6},{5,7},{6,8},{7,9},{8,10},{9,11},{10,... | collective-permute-start | bytes 786440 | tf_op jit(solution)/shard_map/while/body/eval_jaxpr/ppermute | solution.py:17
  530.9 28.5 %collective-permute-start.2 = (f32[128,512]{1,0:T(8,128)S(1)}, f32[128,512]{1,0:T(8,128)S(1)}, u32[]{:S(2)}, u32[]{:S(2)}) collective-permute-start(f32[128,512]{1,0:T(8,128)S(1)} %bitcast.72), channel_id=1, source_target_pairs={{0,16},{1,17},{2,18},{3,19},{4,20},{5,21},{6,22},{7,23},{8,24},{9,... | collective-permute-start | bytes 786440 | tf_op jit(solution)/shard_map/while/body/eval_jaxpr/ppermute | solution.py:23
  590.1 22.3 %collective-permute-start.1 = (f32[128,512]{0,1:T(8,128)S(1)}, f32[128,512]{0,1:T(8,128)}, u32[]{:S(2)}, u32[]{:S(2)}) collective-permute-start(f32[128,512]{0,1:T(8,128)S(1)} %pad_maximum_fusion.8), channel_id=1, source_target_pairs={{0,2},{1,3},{2,4},{3,5},{4,6},{5,7},{6,8},{7,9},{8,10},{9,11},{10,... | collective-permute-start | bytes 786440 | tf_op jit(solution)/shard_map/while/body/eval_jaxpr/ppermute | solution.py:17
  596.5 28.4 %collective-permute-start.2 = (f32[128,512]{1,0:T(8,128)S(1)}, f32[128,512]{1,0:T(8,128)S(1)}, u32[]{:S(2)}, u32[]{:S(2)}) collective-permute-start(f32[128,512]{1,0:T(8,128)S(1)} %bitcast.72), channel_id=1, source_target_pairs={{0,16},{1,17},{2,18},{3,19},{4,20},{5,21},{6,22},{7,23},{8,24},{9,... | collective-permute-start | bytes 786440 | tf_op jit(solution)/shard_map/while/body/eval_jaxpr/ppermute | solution.py:23
  651.8 23.5 %collective-permute-start.1 = (f32[128,512]{0,1:T(8,128)S(1)}, f32[128,512]{0,1:T(8,128)}, u32[]{:S(2)}, u32[]{:S(2)}) collective-permute-start(f32[128,512]{0,1:T(8,128)S(1)} %pad_maximum_fusion.8), channel_id=1, source_target_pairs={{0,2},{1,3},{2,4},{3,5},{4,6},{5,7},{6,8},{7,9},{8,10},{9,11},{10,... | collective-permute-start | bytes 786440 | tf_op jit(solution)/shard_map/while/body/eval_jaxpr/ppermute | solution.py:17
  659.4 25.2 %collective-permute-start.2 = (f32[128,512]{1,0:T(8,128)S(1)}, f32[128,512]{1,0:T(8,128)S(1)}, u32[]{:S(2)}, u32[]{:S(2)}) collective-permute-start(f32[128,512]{1,0:T(8,128)S(1)} %bitcast.72), channel_id=1, source_target_pairs={{0,16},{1,17},{2,18},{3,19},{4,20},{5,21},{6,22},{7,23},{8,24},{9,... | collective-permute-start | bytes 786440 | tf_op jit(solution)/shard_map/while/body/eval_jaxpr/ppermute | solution.py:23
  685.2 22.3 %collective-permute-start.3 = (bf16[128,1024]{1,0:T(8,128)(2,1)S(1)}, bf16[128,1024]{1,0:T(8,128)(2,1)S(1)}, u32[]{:S(2)}, u32[]{:S(2)}) collective-permute-start(bf16[128,1024]{1,0:T(8,128)(2,1)S(1)} %get-tuple-element.560), channel_id=1, source_target_pairs={{0,32},{32,64},{64,96},{96,128},{128,160},{160,192},{192,224},{224... | collective-permute-start | bytes 786440 | tf_op jit(solution)/shard_map/while/body/eval_jaxpr/ppermute | solution.py:17
  718.5 18.6 %collective-permute-start.2 = (f32[128,512]{1,0:T(8,128)S(1)}, f32[128,512]{1,0:T(8,128)S(1)}, u32[]{:S(2)}, u32[]{:S(2)}) collective-permute-start(f32[128,512]{1,0:T(8,128)S(1)} %bitcast.72), channel_id=1, source_target_pairs={{0,16},{1,17},{2,18},{3,19},{4,20},{5,21},{6,22},{7,23},{8,24},{9,... | collective-permute-start | bytes 786440 | tf_op jit(solution)/shard_map/while/body/eval_jaxpr/ppermute | solution.py:23
  756.6 24.0 %collective-permute-start = (f32[128,512]{0,1:T(8,128)S(1)}, f32[128,512]{0,1:T(8,128)S(1)}, u32[]{:S(2)}, u32[]{:S(2)}) collective-permute-start(f32[128,512]{0,1:T(8,128)S(1)} %pad_maximum_fusion.8), channel_id=1, source_target_pairs={{0,1},{1,2},{2,3},{3,4},{4,5},{5,6},{6,7},{7,8},{8,9},{9,10},{10,1... | collective-permute-start | bytes 786440 | tf_op jit(solution)/shard_map/while/body/eval_jaxpr/ppermute | solution.py:17
  762.8 18.7 %collective-permute-start.1 = (f32[128,512]{0,1:T(8,128)S(1)}, f32[128,512]{0,1:T(8,128)}, u32[]{:S(2)}, u32[]{:S(2)}) collective-permute-start(f32[128,512]{0,1:T(8,128)S(1)} %pad_maximum_fusion.8), channel_id=1, source_target_pairs={{0,2},{1,3},{2,4},{3,5},{4,6},{5,7},{6,8},{7,9},{8,10},{9,11},{10,... | collective-permute-start | bytes 786440 | tf_op jit(solution)/shard_map/while/body/eval_jaxpr/ppermute | solution.py:17
  773.1 30.8 %collective-permute-start.2 = (f32[128,512]{1,0:T(8,128)S(1)}, f32[128,512]{1,0:T(8,128)S(1)}, u32[]{:S(2)}, u32[]{:S(2)}) collective-permute-start(f32[128,512]{1,0:T(8,128)S(1)} %bitcast.72), channel_id=1, source_target_pairs={{0,16},{1,17},{2,18},{3,19},{4,20},{5,21},{6,22},{7,23},{8,24},{9,... | collective-permute-start | bytes 786440 | tf_op jit(solution)/shard_map/while/body/eval_jaxpr/ppermute | solution.py:23
  804.5 25.1 %collective-permute-start.3 = (bf16[128,1024]{1,0:T(8,128)(2,1)S(1)}, bf16[128,1024]{1,0:T(8,128)(2,1)S(1)}, u32[]{:S(2)}, u32[]{:S(2)}) collective-permute-start(bf16[128,1024]{1,0:T(8,128)(2,1)S(1)} %get-tuple-element.560), channel_id=1, source_target_pairs={{0,32},{32,64},{64,96},{96,128},{128,160},{160,192},{192,224},{224... | collective-permute-start | bytes 786440 | tf_op jit(solution)/shard_map/while/body/eval_jaxpr/ppermute | solution.py:17
  842.4 25.5 %collective-permute-start.2 = (f32[128,512]{1,0:T(8,128)S(1)}, f32[128,512]{1,0:T(8,128)S(1)}, u32[]{:S(2)}, u32[]{:S(2)}) collective-permute-start(f32[128,512]{1,0:T(8,128)S(1)} %bitcast.72), channel_id=1, source_target_pairs={{0,16},{1,17},{2,18},{3,19},{4,20},{5,21},{6,22},{7,23},{8,24},{9,... | collective-permute-start | bytes 786440 | tf_op jit(solution)/shard_map/while/body/eval_jaxpr/ppermute | solution.py:23
  892.9 20.8 %collective-permute-start.1 = (f32[128,512]{0,1:T(8,128)S(1)}, f32[128,512]{0,1:T(8,128)}, u32[]{:S(2)}, u32[]{:S(2)}) collective-permute-start(f32[128,512]{0,1:T(8,128)S(1)} %pad_maximum_fusion.8), channel_id=1, source_target_pairs={{0,2},{1,3},{2,4},{3,5},{4,6},{5,7},{6,8},{7,9},{8,10},{9,11},{10,... | collective-permute-start | bytes 786440 | tf_op jit(solution)/shard_map/while/body/eval_jaxpr/ppermute | solution.py:17
  901.2 25.4 %collective-permute-start.2 = (f32[128,512]{1,0:T(8,128)S(1)}, f32[128,512]{1,0:T(8,128)S(1)}, u32[]{:S(2)}, u32[]{:S(2)}) collective-permute-start(f32[128,512]{1,0:T(8,128)S(1)} %bitcast.72), channel_id=1, source_target_pairs={{0,16},{1,17},{2,18},{3,19},{4,20},{5,21},{6,22},{7,23},{8,24},{9,... | collective-permute-start | bytes 786440 | tf_op jit(solution)/shard_map/while/body/eval_jaxpr/ppermute | solution.py:23
  942.7 30.0 %collective-permute-start = (f32[128,512]{0,1:T(8,128)S(1)}, f32[128,512]{0,1:T(8,128)S(1)}, u32[]{:S(2)}, u32[]{:S(2)}) collective-permute-start(f32[128,512]{0,1:T(8,128)S(1)} %pad_maximum_fusion.8), channel_id=1, source_target_pairs={{0,1},{1,2},{2,3},{3,4},{4,5},{5,6},{6,7},{7,8},{8,9},{9,10},{10,1... | collective-permute-start | bytes 786440 | tf_op jit(solution)/shard_map/while/body/eval_jaxpr/ppermute | solution.py:17
  947.8 24.9 %collective-permute-start.1 = (f32[128,512]{0,1:T(8,128)S(1)}, f32[128,512]{0,1:T(8,128)}, u32[]{:S(2)}, u32[]{:S(2)}) collective-permute-start(f32[128,512]{0,1:T(8,128)S(1)} %pad_maximum_fusion.8), channel_id=1, source_target_pairs={{0,2},{1,3},{2,4},{3,5},{4,6},{5,7},{6,8},{7,9},{8,10},{9,11},{10,... | collective-permute-start | bytes 786440 | tf_op jit(solution)/shard_map/while/body/eval_jaxpr/ppermute | solution.py:17
  964.0 28.6 %collective-permute-start.2 = (f32[128,512]{1,0:T(8,128)S(1)}, f32[128,512]{1,0:T(8,128)S(1)}, u32[]{:S(2)}, u32[]{:S(2)}) collective-permute-start(f32[128,512]{1,0:T(8,128)S(1)} %bitcast.72), channel_id=1, source_target_pairs={{0,16},{1,17},{2,18},{3,19},{4,20},{5,21},{6,22},{7,23},{8,24},{9,... | collective-permute-start | bytes 786440 | tf_op jit(solution)/shard_map/while/body/eval_jaxpr/ppermute | solution.py:23
  1017.9 22.5 %collective-permute-start.2 = (f32[128,512]{1,0:T(8,128)S(1)}, f32[128,512]{1,0:T(8,128)S(1)}, u32[]{:S(2)}, u32[]{:S(2)}) collective-permute-start(f32[128,512]{1,0:T(8,128)S(1)} %bitcast.72), channel_id=1, source_target_pairs={{0,16},{1,17},{2,18},{3,19},{4,20},{5,21},{6,22},{7,23},{8,24},{9,... | collective-permute-start | bytes 786440 | tf_op jit(solution)/shard_map/while/body/eval_jaxpr/ppermute | solution.py:23
  1041.0 22.5 %collective-permute-start.3 = (bf16[128,1024]{1,0:T(8,128)(2,1)S(1)}, bf16[128,1024]{1,0:T(8,128)(2,1)S(1)}, u32[]{:S(2)}, u32[]{:S(2)}) collective-permute-start(bf16[128,1024]{1,0:T(8,128)(2,1)S(1)} %get-tuple-element.560), channel_id=1, source_target_pairs={{0,32},{32,64},{64,96},{96,128},{128,160},{160,192},{192,224},{224... | collective-permute-start | bytes 786440 | tf_op jit(solution)/shard_map/while/body/eval_jaxpr/ppermute | solution.py:17
  1068.0 21.1 %collective-permute-start = (f32[128,512]{0,1:T(8,128)S(1)}, f32[128,512]{0,1:T(8,128)S(1)}, u32[]{:S(2)}, u32[]{:S(2)}) collective-permute-start(f32[128,512]{0,1:T(8,128)S(1)} %pad_maximum_fusion.8), channel_id=1, source_target_pairs={{0,1},{1,2},{2,3},{3,4},{4,5},{5,6},{6,7},{7,8},{8,9},{9,10},{10,1... | collective-permute-start | bytes 786440 | tf_op jit(solution)/shard_map/while/body/eval_jaxpr/ppermute | solution.py:17
  1085.9 27.5 %collective-permute-start.2 = (f32[128,512]{1,0:T(8,128)S(1)}, f32[128,512]{1,0:T(8,128)S(1)}, u32[]{:S(2)}, u32[]{:S(2)}) collective-permute-start(f32[128,512]{1,0:T(8,128)S(1)} %bitcast.72), channel_id=1, source_target_pairs={{0,16},{1,17},{2,18},{3,19},{4,20},{5,21},{6,22},{7,23},{8,24},{9,... | collective-permute-start | bytes 786440 | tf_op jit(solution)/shard_map/while/body/eval_jaxpr/ppermute | solution.py:23
  1141.0 25.4 %collective-permute-start.2 = (f32[128,512]{1,0:T(8,128)S(1)}, f32[128,512]{1,0:T(8,128)S(1)}, u32[]{:S(2)}, u32[]{:S(2)}) collective-permute-start(f32[128,512]{1,0:T(8,128)S(1)} %bitcast.72), channel_id=1, source_target_pairs={{0,16},{1,17},{2,18},{3,19},{4,20},{5,21},{6,22},{7,23},{8,24},{9,... | collective-permute-start | bytes 786440 | tf_op jit(solution)/shard_map/while/body/eval_jaxpr/ppermute | solution.py:23
  1183.9 20.8 %collective-permute-start = (f32[128,512]{0,1:T(8,128)S(1)}, f32[128,512]{0,1:T(8,128)S(1)}, u32[]{:S(2)}, u32[]{:S(2)}) collective-permute-start(f32[128,512]{0,1:T(8,128)S(1)} %pad_maximum_fusion.8), channel_id=1, source_target_pairs={{0,1},{1,2},{2,3},{3,4},{4,5},{5,6},{6,7},{7,8},{8,9},{9,10},{10,1... | collective-permute-start | bytes 786440 | tf_op jit(solution)/shard_map/while/body/eval_jaxpr/ppermute | solution.py:17
  1199.6 24.5 %collective-permute-start.2 = (f32[128,512]{1,0:T(8,128)S(1)}, f32[128,512]{1,0:T(8,128)S(1)}, u32[]{:S(2)}, u32[]{:S(2)}) collective-permute-start(f32[128,512]{1,0:T(8,128)S(1)} %bitcast.72), channel_id=1, source_target_pairs={{0,16},{1,17},{2,18},{3,19},{4,20},{5,21},{6,22},{7,23},{8,24},{9,... | collective-permute-start | bytes 786440 | tf_op jit(solution)/shard_map/while/body/eval_jaxpr/ppermute | solution.py:23
  1239.9 21.3 %collective-permute-start = (f32[128,512]{0,1:T(8,128)S(1)}, f32[128,512]{0,1:T(8,128)S(1)}, u32[]{:S(2)}, u32[]{:S(2)}) collective-permute-start(f32[128,512]{0,1:T(8,128)S(1)} %pad_maximum_fusion.8), channel_id=1, source_target_pairs={{0,1},{1,2},{2,3},{3,4},{4,5},{5,6},{6,7},{7,8},{8,9},{9,10},{10,1... | collective-permute-start | bytes 786440 | tf_op jit(solution)/shard_map/while/body/eval_jaxpr/ppermute | solution.py:17
  1243.5 19.8 %collective-permute-start.1 = (f32[128,512]{0,1:T(8,128)S(1)}, f32[128,512]{0,1:T(8,128)}, u32[]{:S(2)}, u32[]{:S(2)}) collective-permute-start(f32[128,512]{0,1:T(8,128)S(1)} %pad_maximum_fusion.8), channel_id=1, source_target_pairs={{0,2},{1,3},{2,4},{3,5},{4,6},{5,7},{6,8},{7,9},{8,10},{9,11},{10,... | collective-permute-start | bytes 786440 | tf_op jit(solution)/shard_map/while/body/eval_jaxpr/ppermute | solution.py:17
  1249.1 21.1 %collective-permute-start.2 = (f32[128,512]{1,0:T(8,128)S(1)}, f32[128,512]{1,0:T(8,128)S(1)}, u32[]{:S(2)}, u32[]{:S(2)}) collective-permute-start(f32[128,512]{1,0:T(8,128)S(1)} %bitcast.72), channel_id=1, source_target_pairs={{0,16},{1,17},{2,18},{3,19},{4,20},{5,21},{6,22},{7,23},{8,24},{9,... | collective-permute-start | bytes 786440 | tf_op jit(solution)/shard_map/while/body/eval_jaxpr/ppermute | solution.py:23
  1270.8 23.7 %collective-permute-start.3 = (bf16[128,1024]{1,0:T(8,128)(2,1)S(1)}, bf16[128,1024]{1,0:T(8,128)(2,1)S(1)}, u32[]{:S(2)}, u32[]{:S(2)}) collective-permute-start(bf16[128,1024]{1,0:T(8,128)(2,1)S(1)} %get-tuple-element.560), channel_id=1, source_target_pairs={{0,32},{32,64},{64,96},{96,128},{128,160},{160,192},{192,224},{224... | collective-permute-start | bytes 786440 | tf_op jit(solution)/shard_map/while/body/eval_jaxpr/ppermute | solution.py:17
  1305.7 20.4 %collective-permute-start.2 = (f32[128,512]{1,0:T(8,128)S(1)}, f32[128,512]{1,0:T(8,128)S(1)}, u32[]{:S(2)}, u32[]{:S(2)}) collective-permute-start(f32[128,512]{1,0:T(8,128)S(1)} %bitcast.72), channel_id=1, source_target_pairs={{0,16},{1,17},{2,18},{3,19},{4,20},{5,21},{6,22},{7,23},{8,24},{9,... | collective-permute-start | bytes 786440 | tf_op jit(solution)/shard_map/while/body/eval_jaxpr/ppermute | solution.py:23
  1341.3 32.6 %collective-permute-start = (f32[128,512]{0,1:T(8,128)S(1)}, f32[128,512]{0,1:T(8,128)S(1)}, u32[]{:S(2)}, u32[]{:S(2)}) collective-permute-start(f32[128,512]{0,1:T(8,128)S(1)} %pad_maximum_fusion.8), channel_id=1, source_target_pairs={{0,1},{1,2},{2,3},{3,4},{4,5},{5,6},{6,7},{7,8},{8,9},{9,10},{10,1... | collective-permute-start | bytes 786440 | tf_op jit(solution)/shard_map/while/body/eval_jaxpr/ppermute | solution.py:17
  1355.3 29.4 %collective-permute-start.1 = (f32[128,512]{0,1:T(8,128)S(1)}, f32[128,512]{0,1:T(8,128)}, u32[]{:S(2)}, u32[]{:S(2)}) collective-permute-start(f32[128,512]{0,1:T(8,128)S(1)} %pad_maximum_fusion.8), channel_id=1, source_target_pairs={{0,2},{1,3},{2,4},{3,5},{4,6},{5,7},{6,8},{7,9},{8,10},{9,11},{10,... | collective-permute-start | bytes 786440 | tf_op jit(solution)/shard_map/while/body/eval_jaxpr/ppermute | solution.py:17
  1368.0 26.9 %collective-permute-start.2 = (f32[128,512]{1,0:T(8,128)S(1)}, f32[128,512]{1,0:T(8,128)S(1)}, u32[]{:S(2)}, u32[]{:S(2)}) collective-permute-start(f32[128,512]{1,0:T(8,128)S(1)} %bitcast.72), channel_id=1, source_target_pairs={{0,16},{1,17},{2,18},{3,19},{4,20},{5,21},{6,22},{7,23},{8,24},{9,... | collective-permute-start | bytes 786440 | tf_op jit(solution)/shard_map/while/body/eval_jaxpr/ppermute | solution.py:23
  1395.5 24.3 %collective-permute-start.3 = (bf16[128,1024]{1,0:T(8,128)(2,1)S(1)}, bf16[128,1024]{1,0:T(8,128)(2,1)S(1)}, u32[]{:S(2)}, u32[]{:S(2)}) collective-permute-start(bf16[128,1024]{1,0:T(8,128)(2,1)S(1)} %get-tuple-element.560), channel_id=1, source_target_pairs={{0,32},{32,64},{64,96},{96,128},{128,160},{160,192},{192,224},{224... | collective-permute-start | bytes 786440 | tf_op jit(solution)/shard_map/while/body/eval_jaxpr/ppermute | solution.py:17
  1426.3 23.0 %collective-permute-start.1 = (f32[128,512]{0,1:T(8,128)S(1)}, f32[128,512]{0,1:T(8,128)}, u32[]{:S(2)}, u32[]{:S(2)}) collective-permute-start(f32[128,512]{0,1:T(8,128)S(1)} %pad_maximum_fusion.8), channel_id=1, source_target_pairs={{0,2},{1,3},{2,4},{3,5},{4,6},{5,7},{6,8},{7,9},{8,10},{9,11},{10,... | collective-permute-start | bytes 786440 | tf_op jit(solution)/shard_map/while/body/eval_jaxpr/ppermute | solution.py:17
  1429.5 29.3 %collective-permute-start.2 = (f32[128,512]{1,0:T(8,128)S(1)}, f32[128,512]{1,0:T(8,128)S(1)}, u32[]{:S(2)}, u32[]{:S(2)}) collective-permute-start(f32[128,512]{1,0:T(8,128)S(1)} %bitcast.72), channel_id=1, source_target_pairs={{0,16},{1,17},{2,18},{3,19},{4,20},{5,21},{6,22},{7,23},{8,24},{9,... | collective-permute-start | bytes 786440 | tf_op jit(solution)/shard_map/while/body/eval_jaxpr/ppermute | solution.py:23
  1476.9 21.5 %collective-permute-start.2 = (f32[128,512]{1,0:T(8,128)S(1)}, f32[128,512]{1,0:T(8,128)S(1)}, u32[]{:S(2)}, u32[]{:S(2)}) collective-permute-start(f32[128,512]{1,0:T(8,128)S(1)} %bitcast.72), channel_id=1, source_target_pairs={{0,16},{1,17},{2,18},{3,19},{4,20},{5,21},{6,22},{7,23},{8,24},{9,... | collective-permute-start | bytes 786440 | tf_op jit(solution)/shard_map/while/body/eval_jaxpr/ppermute | solution.py:23
  1498.9 18.8 %collective-permute-start.3 = (bf16[128,1024]{1,0:T(8,128)(2,1)S(1)}, bf16[128,1024]{1,0:T(8,128)(2,1)S(1)}, u32[]{:S(2)}, u32[]{:S(2)}) collective-permute-start(bf16[128,1024]{1,0:T(8,128)(2,1)S(1)} %get-tuple-element.560), channel_id=1, source_target_pairs={{0,32},{32,64},{64,96},{96,128},{128,160},{160,192},{192,224},{224... | collective-permute-start | bytes 786440 | tf_op jit(solution)/shard_map/while/body/eval_jaxpr/ppermute | solution.py:17
  (72 other events, 743.3 us)
